TPU v7x, 32 devices: a whole 2x2x4 slice. The times are simulated.
32 devices in a mesh: section: 16 (over z, y, core), dp: 2 (over x).
Axes of the slice: x: 2, y: 2, z: 4, core: 2. Of those that a mesh axis runs over, the one named last changes fastest.
Arguments:
- activations: bfloat16 [2, 16, 2, 8, 32, 416], P(None, 'section', 'dp'), may hold values from -6 to 6
- stored_inputs: bfloat16 [2, 3, 16, 2, 8, 32, 416], P(None, None, 'section', 'dp'), may hold values from -6 to 6
- cotangents: bfloat16 [2, 16, 2, 8, 32, 416], P(None, 'section', 'dp'), may hold values from -6 to 6
- new_inputs: bfloat16 [2, 2, 2, 8, 32, 416], P(None, None, 'dp'), may hold values from -6 to 6
- loss_grad: bfloat16 [2, 2, 2, 8, 32, 416], P(None, None, 'dp'), may hold values from -6 to 6
- depth_kernel: bfloat16 [16, 2, 1, 5, 5, 416], P('section'), may hold values from -1.25 to 1.25
- depth_bias: float32 [16, 2, 1, 416], P('section'), may hold values from -3 to 3
- mixing: bfloat16 [16, 2, 1, 416, 416], P('section'), may hold values from -0.3125 to 0.3125
Outputs:
- section_outputs: bfloat16 [2, 16, 2, 8, 32, 416], P(None, 'section', 'dp')
- input_grads: bfloat16 [2, 16, 2, 8, 32, 416], P(None, 'section', 'dp')
- grad_kernel: float32 [16, 1, 5, 5, 416], P('section', None, None, None, 'dp')
- grad_bias: float32 [16, 1, 416], P('section', None, 'dp')
- grad_mixing: float32 [16, 1, 416, 416], P('section', None, 'dp')
All inputs are finite; a program needn't handle non-finite values.
Results may differ from a plain program's by a relative error of at most 0.0062.
Values may be sent and summed in bfloat16 or wider, within the bound.
A program may use at most 128 MiB of HBM per device.

v0:
```python
import functools
import math

import jax
import jax.numpy as jnp
from jax import lax
from jax.experimental import pallas as pl
from jax.experimental.pallas import tpu as pltpu
from jax.sharding import PartitionSpec as P

LANES = 128
SUB = 8
GELU_A = math.sqrt(2.0 / math.pi)
GELU_B = GELU_A * 0.044715
MESH = pl.DeviceIdType.MESH


def relay_kernel(
    n, act, cot, new_in, loss, stored, kern, bias, mix,
    y_out, dx_out, dp_out, dk_out,
    xf, xb, dpad, hid, hidb, slope, work, kw, dk_acc, rx, tx,
    local_sem, send_sem, recv_sem, out_sem,
):
    ticks = stored.shape[1]
    height, width, chans = stored.shape[-3:]
    side = kern.shape[-2]
    margin = side // 2
    tiles = xf.shape[0]
    taps = side * side
    widths = [min(LANES, chans - t * LANES) for t in range(tiles)]
    pos = lax.axis_index("section")
    right, left = lax.rem(pos + 1, n), lax.rem(pos + n - 1, n)

    for c in range(4):
        first = (act if c < 2 else cot).at[c % 2, 0, 0]
        pltpu.make_async_copy(first, rx.at[0, c], local_sem.at[0, c]).start()
    for c, entry in ((0, 0), (1, n - 1), (2, n - 1), (3, 0)):
        @pl.when(pos == entry)
        def _():
            for t in range(1, ticks):
                source = (new_in if c < 2 else loss).at[c % 2, t - 1, 0]
                pltpu.make_async_copy(source, rx.at[t, c], local_sem.at[t, c]).start()

    barrier = pltpu.get_barrier_semaphore()
    for other in (left, right):
        pl.semaphore_signal(barrier, inc=1, device_id={"section": other}, device_id_type=MESH)

    xf[...] = jnp.zeros(xf.shape, jnp.float32)
    xb[...] = jnp.zeros(xb.shape, jnp.float32)
    dpad[...] = jnp.zeros(dpad.shape, jnp.float32)
    dk_acc[...] = jnp.zeros(dk_acc.shape, jnp.float32)
    dp_out[...] = jnp.zeros(dp_out.shape, jnp.float32)
    kw[...] = jnp.zeros(kw.shape, jnp.float32)
    for r in range(2):
        for l, wide in enumerate(widths):
            lanes = slice(l * LANES, l * LANES + wide)
            for a in range(side):
                kw[r, l, a * side : (a + 1) * side, :wide] = kern[0, r, 0, a, :, lanes].astype(jnp.float32)
            kw[r, l, taps : taps + 1, :wide] = bias[0, r, :, lanes]
    pl.semaphore_wait(barrier, 2)

    def stage(source, dest):
        for l, wide in enumerate(widths):
            values = source[:, :, l * LANES : l * LANES + wide].astype(jnp.float32)
            dest[l, :, SUB : SUB + width, :wide] = values

    def shifted(ref, h, b):
        start = SUB - margin + b
        return ref[h, start : start + width, :]

    def conv(ref, r, l, flip, init):
        total = [init] * height
        for b in range(side):
            row = []
            for a in range(side):
                place = taps - 1 - (a * side + b) if flip else a * side + b
                row.append(jnp.broadcast_to(kw[r, l, place : place + 1, :], (width, LANES)))
            for source in range(height):
                values = shifted(ref, source, b)
                for a in range(side):
                    h = source - a + margin
                    if 0 <= h < height:
                        total[h] = total[h] + values * row[a]
        return total

    def rows(h):
        return pl.ds(h * width, width)

    def lane_tile(l):
        return pl.ds(pl.multiple_of(l * LANES, LANES), LANES)

    def link(t, c, dst):
        return pltpu.make_async_remote_copy(
            src_ref=tx.at[t, c],
            dst_ref=rx.at[t + 1, c],
            send_sem=send_sem.at[t, c],
            recv_sem=recv_sem.at[t + 1, c],
            device_id={"section": dst},
            device_id_type=MESH,
        )

    def inside(place):
        return jnp.logical_and(place >= 0, place < n)

    def arrive(t, c, src):
        remote = jnp.logical_and(t > 0, inside(src))

        @pl.when(remote)
        def _():
            pltpu.make_async_remote_copy(
                src_ref=tx.at[t, c],
                dst_ref=rx.at[t, c],
                send_sem=send_sem.at[t, c],
                recv_sem=recv_sem.at[t, c],
                device_id={"section": left},
                device_id_type=MESH,
            ).wait_recv()

        @pl.when(jnp.logical_not(remote))
        def _():
            pltpu.make_async_copy(act.at[0, 0, 0], rx.at[t, c], local_sem.at[t, c]).wait()

    def depart(t, c, dst):
        @pl.when(jnp.logical_and(t < ticks - 1, inside(dst)))
        def _():
            link(t, c, dst).start()

    def forward(r, t):
        arrive(t, r, pos - 1 + 2 * r)
        stage(rx.at[t, r], xf)

        def tile(l, carry):
            first = jnp.broadcast_to(kw[r, l, taps : taps + 1, :], (width, LANES))
            total = conv(xf.at[l], r, l, False, first)
            for h in range(height):
                u = total[h]
                half = 0.5 * u
                th = jnp.tanh(u * (GELU_A + GELU_B * (u * u)))
                hid[rows(h), lane_tile(l)] = (half + half * th).astype(jnp.bfloat16)
            return carry

        lax.fori_loop(0, tiles, tile, 0)
        mixed = jnp.dot(hid[:, :chans], mix[0, r, 0], preferred_element_type=jnp.float32)
        result = rx[t, r].astype(jnp.float32) + mixed.reshape(height, width, chans)
        tx[t, r] = result.astype(jnp.bfloat16)
        depart(t, r, pos + 1 - 2 * r)

    def backward(r, t):
        stage(stored.at[r, t, 0, 0], xb.at[r])

        def tile(l, carry):
            first = jnp.broadcast_to(kw[r, l, taps : taps + 1, :], (width, LANES))
            total = conv(xb.at[r, l], r, l, False, first)
            for h in range(height):
                u = total[h]
                half = 0.5 * u
                square = u * u
                th = jnp.tanh(u * (GELU_A + GELU_B * square))
                hidb[r, rows(h), lane_tile(l)] = (half + half * th).astype(jnp.bfloat16)
                inner = GELU_A + (3.0 * GELU_B) * square
                slope[l, rows(h), :] = (0.5 + 0.5 * th) + half * (1.0 - th * th) * inner
            return carry

        lax.fori_loop(0, tiles, tile, 0)
        arrive(t, 2 + r, pos + 1 - 2 * r)
        incoming = rx[t, 2 + r].reshape(height * width, chans)
        work[:, :chans] = lax.dot_general(
            incoming, mix[0, r, 0], (((1,), (1,)), ((), ())), preferred_element_type=jnp.float32
        )

        def spread(l, carry):
            bias_sum = jnp.zeros((SUB, LANES), jnp.float32)
            for h in range(height):
                grad = work[rows(h), lane_tile(l)] * slope[l, rows(h), :]
                dpad[r, l, h, SUB : SUB + width, :] = grad
                for w in range(0, width, SUB):
                    bias_sum = bias_sum + grad[w : w + SUB]
            dk_acc[r, l, taps] = dk_acc[r, l, taps] + bias_sum
            total = conv(dpad.at[r, l], r, l, True, jnp.zeros((width, LANES), jnp.float32))
            for h in range(height):
                work[rows(h), lane_tile(l)] = total[h]
            return carry

        lax.fori_loop(0, tiles, spread, 0)
        result = rx[t, 2 + r].astype(jnp.float32) + work[:, :chans].reshape(height, width, chans)
        tx[t, 2 + r] = result.astype(jnp.bfloat16)
        depart(t, 2 + r, pos - 1 + 2 * r)

    def weights(r, t):
        incoming = rx[t, 2 + r].reshape(height * width, chans)
        dp_out[r] += lax.dot_general(
            hidb[r, :, :chans], incoming, (((0,), (0,)), ((), ())), preferred_element_type=jnp.float32
        )

        def tile(l, carry):
            grads = [dpad[r, l, h, SUB : SUB + width, :] for h in range(height)]
            for b in range(side):
                sums = [None] * side
                for source in range(height):
                    values = shifted(xb.at[r, l], source, b)
                    for a in range(side):
                        h = source - a + margin
                        if 0 <= h < height:
                            product = grads[h] * values
                            for w in range(0, width, SUB):
                                part = product[w : w + SUB]
                                sums[a] = part if sums[a] is None else sums[a] + part
                for a in range(side):
                    dk_acc[r, l, a * side + b] = dk_acc[r, l, a * side + b] + sums[a]
            return carry

        lax.fori_loop(0, tiles, tile, 0)

    def over_replicas(step, t):
        def one(r, carry):
            step(r, t)
            return carry

        lax.fori_loop(0, 2, one, 0)

    def tick(t, carry):
        over_replicas(forward, t)
        over_replicas(backward, t)
        over_replicas(weights, t)
        return carry

    lax.fori_loop(0, ticks, tick, 0)

    outs = []
    for c in range(4):
        target = (y_out if c < 2 else dx_out).at[c % 2, 0, 0]
        copy = pltpu.make_async_copy(tx.at[ticks - 1, c], target, out_sem.at[c])
        copy.start()
        outs.append(copy)
    for r in range(2):
        for l, wide in enumerate(widths):
            total = jnp.sum(dk_acc[r, l], axis=1)
            dk_out[r, : taps + 1, l * LANES : l * LANES + wide] = total[:, :wide]
    for t in range(ticks - 1):
        for c, step in ((0, 1), (1, -1), (2, -1), (3, 1)):
            @pl.when(inside(pos + step))
            def _():
                link(t, c, pos + step).wait_send()
    for copy in outs:
        copy.wait()


def relay(n, act, cot, new_in, loss, stored, kern, bias, mix):
    ticks = stored.shape[1]
    height, width, chans = stored.shape[-3:]
    side = kern.shape[-2]
    taps = side * side
    tiles = -(-chans // LANES)
    padded = tiles * LANES
    count = height * width
    across = width + 2 * SUB
    f32, bf16 = jnp.float32, jnp.bfloat16
    vmem = pl.BlockSpec(memory_space=pltpu.VMEM)
    anywhere = pl.BlockSpec(memory_space=pl.ANY)
    small = -(-(taps + 1) // SUB) * SUB
    return pl.pallas_call(
        functools.partial(relay_kernel, n),
        out_shape=(
            jax.ShapeDtypeStruct(act.shape, bf16),
            jax.ShapeDtypeStruct(cot.shape, bf16),
            jax.ShapeDtypeStruct((2, chans, chans), f32),
            jax.ShapeDtypeStruct((2, taps + 1, chans), f32),
        ),
        in_specs=[anywhere] * 4 + [vmem] * 4,
        out_specs=(anywhere, anywhere, vmem, vmem),
        scratch_shapes=[
            pltpu.VMEM((tiles, height, across, LANES), f32),
            pltpu.VMEM((2, tiles, height, across, LANES), f32),
            pltpu.VMEM((2, tiles, height, across, LANES), f32),
            pltpu.VMEM((count, padded), bf16),
            pltpu.VMEM((2, count, padded), bf16),
            pltpu.VMEM((tiles, count, LANES), f32),
            pltpu.VMEM((count, padded), f32),
            pltpu.VMEM((2, tiles, small, LANES), f32),
            pltpu.VMEM((2, tiles, taps + 1, SUB, LANES), f32),
            pltpu.VMEM((ticks, 4, height, width, chans), bf16),
            pltpu.VMEM((ticks, 4, height, width, chans), bf16),
            pltpu.SemaphoreType.DMA((ticks, 4)),
            pltpu.SemaphoreType.DMA((ticks, 4)),
            pltpu.SemaphoreType.DMA((ticks, 4)),
            pltpu.SemaphoreType.DMA((4,)),
        ],
        compiler_params=pltpu.CompilerParams(
            collective_id=0, has_side_effects=True, vmem_limit_bytes=40 * 1024 * 1024
        ),
        name="relay",
    )(act, cot, new_in, loss, stored, kern, bias, mix)


def per_device(
    activations, stored_inputs, cotangents, new_inputs, loss_grad, depth_kernel, depth_bias, mixing
):
    sections = lax.axis_size("section")
    side = depth_kernel.shape[-2]
    taps = side * side
    ticks = stored_inputs.shape[1]
    outputs, grads, mix_sums, small_sums = relay(
        sections, activations, cotangents, new_inputs, loss_grad,
        stored_inputs, depth_kernel, depth_bias, mixing,
    )
    mix_share = lax.psum_scatter(mix_sums, "dp", scatter_dimension=1, tiled=True)
    small_share = lax.psum_scatter(small_sums, "dp", scatter_dimension=2, tiled=True)
    swap = [(i, sections - 1 - i) for i in range(sections)]
    mix_other, small_other = lax.ppermute((mix_share[1], small_share[1]), "section", swap)
    map_rows = activations.shape[3] * activations.shape[4]
    factor = (2.0 * ticks * activations.shape[2] * lax.axis_size("dp") * map_rows) ** (-0.5)
    grad_mixing = ((mix_share[0] + mix_other) * factor)[None, None]
    small = (small_share[0] + small_other) * factor
    grad_kernel = small[:taps].reshape(1, 1, side, side, -1)
    grad_bias = small[taps][None, None]
    return (outputs, grads, grad_kernel, grad_bias, grad_mixing)


def solution(mesh):
    return jax.shard_map(
        per_device,
        mesh=mesh,
        in_specs=(
            P(None, "section", "dp", None, None, None),
            P(None, None, "section", "dp", None, None, None),
            P(None, "section", "dp", None, None, None),
            P(None, None, "dp", None, None, None),
            P(None, None, "dp", None, None, None),
            P("section", None, None, None, None, None),
            P("section", None, None, None),
            P("section", None, None, None, None),
        ),
        out_specs=(
            P(None, "section", "dp", None, None, None),
            P(None, "section", "dp", None, None, None),
            P("section", None, None, None, "dp"),
            P("section", None, "dp"),
            P("section", None, "dp", None),
        ),
        check_vma=False,
    )
```

profile of v0, /device:TPU:9, one launch (start us, length us, event | category | flops | bytes accessed | tf_op | source)
XLA Modules:
  0.0 127.9 jit_solution(12050521384431993669)
XLA Ops:
  7.2 0.0 reduce-scatter.7.cloned.1.call-start
  7.2 0.8 copy.17.kern
  8.0 0.0 copy-start
  8.0 1.4 %copy-done = bf16[2,3,1,1,8,32,416]{6,5,4,3,2,1,0:T(8,128)(2,1)S(1)} copy-done((bf16[2,3,1,1,8,32,416]{6,5,4,3,2,1,0:T(8,128)(2,1)S(1)}, bf16[2,3,1,1,8,32,416]{6,5,4,3,2,1,0:T(8,128)(2,1)}, u32[]{:S(2)}) %copy-start) | copy-done | bytes 1277976
  9.4 0.0 copy-start.1
  9.4 1.2 copy-done.1
  10.7 0.0 copy-start.2
  10.7 1.2 copy-done.2
  11.9 0.0 copy-start.3
  11.9 1.2 copy-done.3
  13.1 0.0 copy-start.4
  13.1 1.0 copy-done.4
  14.1 0.0 copy-start.5
  14.1 1.0 copy-done.5
  15.1 0.0 copy-start.6
  15.1 0.7 copy-done.6
  15.8 36.4 %relay.1 = (bf16[2,1,1,8,32,416]{5,4,3,2,1,0:T(8,128)(2,1)S(1)}, bf16[2,1,1,8,32,416]{5,4,3,2,1,0:T(8,128)(2,1)S(1)}, f32[2,416,416]{2,1,0:T(8,128)}, f32[2,26,416]{2,1,0:T(8,128)S(1)}) custom-call(bf16[2,1,1,8,32,416]{5,4,3,2,1,0:T(8,128)(2,1)S(1)} %copy-done.4, bf16[2,1,1,8,32,416]{5,4,3,2,1,0:T(8,128)(2,1)S(1)} %copy-done.5, ...), custom_call_target="tpu_custom_call" | custom-call | tf_op jit(solution)/shard_map/relay/pallas_call | solution.py:261
  52.2 0.2 copy.19
  52.5 0.9 reshape.14
  53.4 0.0 reduce-scatter.7.cloned.1.call-update
  53.4 0.0 reduce-scatter.5.cloned.1.call-start
  53.5 0.7 reduce-scatter.5.cloned.1.call-update
  54.2 10.2 %reduce-scatter.7.cloned.1.call-done = f32[208,52]{1,0:T(8,128)} async-done(((f32[416,52]{1,0:T(8,128)}), f32[208,52]{1,0:T(8,128)}) %reduce-scatter.7.cloned.1.call-update) | async-done | bytes 43280
  64.4 1.1 reshape.15
  65.5 0.2 fusion.4
  65.6 0.1 copy.22
  65.7 2.7 %collective-permute-start = (f32[26,208]{1,0:T(8,128)S(1)}, f32[26,208]{1,0:T(8,128)S(1)}, u32[]{:S(2)}, u32[]{:S(2)}) collective-permute-start(f32[26,208]{1,0:T(8,128)S(1)} %bitcast.25), channel_id=1, source_target_pairs={{0,30},{2,28},{4,26},{6,24},{8,22},{10,20},{12,18},{14,16},{16,14}... | collective-permute-start | bytes 64904 | tf_op jit(solution)/shard_map/ppermute | solution.py:309
  68.4 0.1 copy.21
  68.5 25.7 %reduce-scatter.5.cloned.1.call-done = f32[2,208,416]{2,1,0:T(8,128)} async-done(((f32[2,416,416]{2,1,0:T(8,128)}), f32[2,208,416]{2,1,0:T(8,128)}) %reduce-scatter.5.cloned.1.call-update) | async-done | bytes 692240 | tf_op jit(solution)/shard_map/reduce_scatter | solution.py:306
  94.2 1.0 slice_bitcast_fusion
  95.2 2.7 %collective-permute-start.1 = (f32[208,416]{1,0:T(8,128)S(1)}, f32[208,416]{1,0:T(8,128)S(1)}, u32[]{:S(2)}, u32[]{:S(2)}) collective-permute-start(f32[208,416]{1,0:T(8,128)S(1)} %slice_bitcast_fusion), channel_id=1, source_target_pairs={{0,30},{2,28},{4,26},{6,24},{8,22},{10,20},{12,18},{14,16},{16,14}... | collective-permute-start | bytes 1038344 | tf_op jit(solution)/shard_map/ppermute | solution.py:309
  98.0 0.0 collective-permute-done
  98.0 0.6 reshape.16
  98.6 0.6 slice_bitcast_fusion.2
  99.2 18.5 %collective-permute-done.1 = f32[208,416]{1,0:T(8,128)S(1)} collective-permute-done((f32[208,416]{1,0:T(8,128)S(1)}, f32[208,416]{1,0:T(8,128)S(1)}, u32[]{:S(2)}, u32[]{:S(2)}) %collective-permute-start.1) | collective-permute-done | bytes 346144 | tf_op jit(solution)/shard_map/ppermute | solution.py:309
  117.7 1.8 %fusion.2 = f32[1,1,208,416]{3,2,1,0:T(8,128)} fusion(f32[208,416]{1,0:T(8,128)S(1)} %collective-permute-done.1, f32[2,208,416]{2,1,0:T(8,128)} %reduce-scatter.5.cloned.1.call-done), kind=kLoop, calls=%fused_computation.4 | loop fusion | flops 173056 | bytes 1038336 | tf_op jit(solution)/shard_map/broadcast_in_dim | solution.py:312
  119.5 0.8 copy.25
  120.3 0.8 copy.26
  (1 shorter events, 0.0 us)
Async XLA Ops:
  7.2 57.2 %reduce-scatter.7.cloned.1.call-start = ((), (), s32[]{:S(2)}) async-start(), calls=%async_computation.3 | async-start | bytes 319488
  8.0 1.4 %copy-start = (bf16[2,3,1,1,8,32,416]{6,5,4,3,2,1,0:T(8,128)(2,1)S(1)}, bf16[2,3,1,1,8,32,416]{6,5,4,3,2,1,0:T(8,128)(2,1)}, u32[]{:S(2)}) copy-start(bf16[2,3,1,1,8,32,416]{6,5,4,3,2,1,0:T(8,128)(2,1)} %stored.1) | copy-start | bytes 3833860
  9.4 1.2 copy-start.1
  10.7 1.2 copy-start.2
  11.9 1.2 copy-start.3
  13.1 1.0 copy-start.4
  14.1 1.0 copy-start.5
  15.1 0.7 copy-start.6
  53.4 40.8 %reduce-scatter.5.cloned.1.call-start = ((), (), s32[]{:S(2)}) async-start(), calls=%async_computation.2 | async-start | bytes 2555904 | tf_op jit(solution)/shard_map/reduce_scatter | solution.py:306
  65.7 32.3 %collective-permute-start = (f32[26,208]{1,0:T(8,128)S(1)}, f32[26,208]{1,0:T(8,128)S(1)}, u32[]{:S(2)}, u32[]{:S(2)}) collective-permute-start(f32[26,208]{1,0:T(8,128)S(1)} %bitcast.25), channel_id=1, source_target_pairs={{0,30},{2,28},{4,26},{6,24},{8,22},{10,20},{12,18},{14,16},{16,14}... | collective-permute-start | bytes 64904 | tf_op jit(solution)/shard_map/ppermute | solution.py:309
  95.2 22.5 %collective-permute-start.1 = (f32[208,416]{1,0:T(8,128)S(1)}, f32[208,416]{1,0:T(8,128)S(1)}, u32[]{:S(2)}, u32[]{:S(2)}) collective-permute-start(f32[208,416]{1,0:T(8,128)S(1)} %slice_bitcast_fusion), channel_id=1, source_target_pairs={{0,30},{2,28},{4,26},{6,24},{8,22},{10,20},{12,18},{14,16},{16,14}... | collective-permute-start | bytes 1038344 | tf_op jit(solution)/shard_map/ppermute | solution.py:309
Sparse Core Ops, SparseCore 0:
  53.5 10.7 reduce-scatter.6
  66.6 27.5 reduce-scatter.4
where the time goes:
time: 128 us
  waiting for transfers between devices  55.1 us (43%)
  Pallas kernels  36.4 us (28%)
  local copies, waits for them, and re-layouts  15 us (12%)
  between operations  14.1 us (11%)
  starting transfers between devices  5.55 us (4%)
  other arithmetic  1.84 us (1%)
    pallas_call x1, Pallas kernels, relay(): pl.pallas_call(functools.partial(relay_kernel, n), out_shape=(jax.ShapeDt...  36.4 us
    reduce_scatter x1, waiting for transfers between devices, per_device(): lax.psum_scatter(mix_sums, 'dp', scatter_dimension=1, tiled=True)  25.7 us
    ppermute x2, waiting for transfers between devices, per_device(): lax.ppermute((mix_share[1], small_share[1]), 'section', swap)  18.5 us
    unnamed x22, local copies, waits for them, and re-layouts  12.6 us
    unnamed x3, waiting for transfers between devices  10.9 us
    ppermute x2, starting transfers between devices, per_device(): lax.ppermute((mix_share[1], small_share[1]), 'section', swap)  5.47 us
  transfers between devices with their start and end apart: 4, of which 3 were waited for; matrix products, arithmetic and copies ran while one was open for 3% of the time, Pallas kernels for 0%

commit v1 on v0

--- a/solution.py
+++ b/solution.py
@@ -16,14 +16,18 @@
 
 
 def relay_kernel(
-    n, act, cot, new_in, loss, stored, kern, bias, mix,
-    y_out, dx_out, dp_out, dk_out,
-    xf, xb, dpad, hid, hidb, slope, work, kw, dk_acc, rx, tx,
-    local_sem, send_sem, recv_sem, out_sem,
+    n, share, factor, act, cot, new_in, loss, stored_in, kern_in, bias_in, mix_in, *refs
 ):
+    outs, refs = refs[:4 + (share > 0)], refs[4 + (share > 0):]
+    y_out, dx_out = outs[:2]
+    (
+        xf, xb, dpad, hid, hidb, slope, work, kw, dk_acc, dp_acc, small, rx, tx,
+        stored, kern, bias, mix, parcel, landed,
+        local_sem, send_sem, recv_sem, out_sem, load_sem, stored_sem, swap_send, swap_recv,
+    ) = refs
     ticks = stored.shape[1]
     height, width, chans = stored.shape[-3:]
-    side = kern.shape[-2]
+    side = kern.shape[2]
     margin = side // 2
     tiles = xf.shape[0]
     taps = side * side
@@ -31,9 +35,20 @@
     pos = lax.axis_index("section")
     right, left = lax.rem(pos + 1, n), lax.rem(pos + n - 1, n)
 
+    loads = [
+        pltpu.make_async_copy(source, dest, load_sem.at[i])
+        for i, (source, dest) in enumerate(((kern_in, kern), (bias_in, bias), (mix_in, mix)))
+    ]
+    for load in loads:
+        load.start()
+    pltpu.make_async_copy(stored_in.at[1, 0], stored.at[1, 0], stored_sem.at[1, 0]).start()
     for c in range(4):
         first = (act if c < 2 else cot).at[c % 2, 0, 0]
         pltpu.make_async_copy(first, rx.at[0, c], local_sem.at[0, c]).start()
+    for t in range(ticks):
+        for r in (1, 0):
+            if (r, t) != (1, 0):
+                pltpu.make_async_copy(stored_in.at[r, t], stored.at[r, t], stored_sem.at[r, t]).start()
     for c, entry in ((0, 0), (1, n - 1), (2, n - 1), (3, 0)):
         @pl.when(pos == entry)
         def _():
@@ -42,22 +57,34 @@
                 pltpu.make_async_copy(source, rx.at[t, c], local_sem.at[t, c]).start()
 
     barrier = pltpu.get_barrier_semaphore()
-    for other in (left, right):
-        pl.semaphore_signal(barrier, inc=1, device_id={"section": other}, device_id_type=MESH)
-
-    xf[...] = jnp.zeros(xf.shape, jnp.float32)
-    xb[...] = jnp.zeros(xb.shape, jnp.float32)
-    dpad[...] = jnp.zeros(dpad.shape, jnp.float32)
+    greeted = [{"section": left}, {"section": right}]
+    if share:
+        half = lax.axis_index("dp")
+        peer, mirror = {"dp": 1 - half}, {"section": n - 1 - pos}
+        greeted += [peer, mirror]
+    for other in greeted:
+        pl.semaphore_signal(barrier, inc=1, device_id=other, device_id_type=MESH)
+
+    for ref in (xf, xb, dpad):
+        edge = jnp.zeros(ref.shape[:-2] + (SUB, LANES), jnp.float32)
+        ref[..., :SUB, :] = edge
+        ref[..., SUB + width :, :] = edge
     dk_acc[...] = jnp.zeros(dk_acc.shape, jnp.float32)
-    dp_out[...] = jnp.zeros(dp_out.shape, jnp.float32)
-    kw[...] = jnp.zeros(kw.shape, jnp.float32)
-    for r in range(2):
-        for l, wide in enumerate(widths):
-            lanes = slice(l * LANES, l * LANES + wide)
-            for a in range(side):
-                kw[r, l, a * side : (a + 1) * side, :wide] = kern[0, r, 0, a, :, lanes].astype(jnp.float32)
-            kw[r, l, taps : taps + 1, :wide] = bias[0, r, :, lanes]
-    pl.semaphore_wait(barrier, 2)
+    dp_acc[...] = jnp.zeros(dp_acc.shape, jnp.float32)
+    small[...] = jnp.zeros(small.shape, jnp.float32)
+    for load in loads:
+        load.wait()
+    for a in range(side):
+        for b in range(side):
+            pair = kern[0, 0, a, b].astype(jnp.float32)
+            place = a * side + b
+            for l, wide in enumerate(widths):
+                for r in range(2):
+                    kw[r, l, place : place + 1, :wide] = pair[r : r + 1, l * LANES : l * LANES + wide]
+    for l, wide in enumerate(widths):
+        for r in range(2):
+            kw[r, l, taps : taps + 1, :wide] = bias[0, r, :, l * LANES : l * LANES + wide]
+    pl.semaphore_wait(barrier, len(greeted))
 
     def stage(source, dest):
         for l, wide in enumerate(widths):
@@ -146,6 +173,7 @@
         depart(t, r, pos + 1 - 2 * r)
 
     def backward(r, t):
+        pltpu.make_async_copy(stored_in.at[r, t], stored.at[r, t], stored_sem.at[r, t]).wait()
         stage(stored.at[r, t, 0, 0], xb.at[r])
 
         def tile(l, carry):
@@ -188,7 +216,7 @@
 
     def weights(r, t):
         incoming = rx[t, 2 + r].reshape(height * width, chans)
-        dp_out[r] += lax.dot_general(
+        dp_acc[r] += lax.dot_general(
             hidb[r, :, :chans], incoming, (((0,), (0,)), ((), ())), preferred_element_type=jnp.float32
         )
 
@@ -211,44 +239,96 @@
 
         lax.fori_loop(0, tiles, tile, 0)
 
-    def over_replicas(step, t):
-        def one(r, carry):
-            step(r, t)
-            return carry
-
-        lax.fori_loop(0, 2, one, 0)
+    def finish_small(r):
+        for l, wide in enumerate(widths):
+            total = jnp.sum(dk_acc[r, l], axis=1)
+            small[r, : taps + 1, l * LANES : l * LANES + wide] = total[:, :wide]
+
+    if share:
+        swaps = [
+            pltpu.make_async_remote_copy(
+                src_ref=parcel.at[i],
+                dst_ref=landed.at[i],
+                send_sem=swap_send.at[i],
+                recv_sem=swap_recv.at[i],
+                device_id=mirror if i == 2 else peer,
+                device_id_type=MESH,
+            )
+            for i in range(3)
+        ]
+
+    def mix_half(r, which):
+        return dp_acc[r, pl.ds(pl.multiple_of(which * share, SUB), share), :]
+
+    def small_half(r, which):
+        return jnp.where(which == 0, small[r, :, :share], small[r, :, share:])
+
+    def send_half(r):
+        finish_small(r)
+        parcel[r, :share, :] = mix_half(r, 1 - half).astype(jnp.bfloat16)
+        parcel[r, share:, :share] = small_half(r, 1 - half).astype(jnp.bfloat16)
+        swaps[r].start()
+
+    def send_mirror():
+        swaps[1].wait_recv()
+        mixed = mix_half(1, half) + landed[1, :share, :].astype(jnp.float32)
+        parcel[2, :share, :] = mixed.astype(jnp.bfloat16)
+        rest = small_half(1, half) + landed[1, share:, :share].astype(jnp.float32)
+        parcel[2, share:, :share] = rest.astype(jnp.bfloat16)
+        swaps[2].start()
 
     def tick(t, carry):
-        over_replicas(forward, t)
-        over_replicas(backward, t)
-        over_replicas(weights, t)
+        last = t == ticks - 1
+        for r in (1, 0):
+            backward(r, t)
+            if share and r == 0:
+                pl.when(last)(send_mirror)
+            weights(r, t)
+            if share:
+                pl.when(last)(functools.partial(send_half, r))
+        for r in (0, 1):
+            forward(r, t)
         return carry
 
     lax.fori_loop(0, ticks, tick, 0)
 
-    outs = []
+    done = []
     for c in range(4):
         target = (y_out if c < 2 else dx_out).at[c % 2, 0, 0]
         copy = pltpu.make_async_copy(tx.at[ticks - 1, c], target, out_sem.at[c])
         copy.start()
-        outs.append(copy)
-    for r in range(2):
-        for l, wide in enumerate(widths):
-            total = jnp.sum(dk_acc[r, l], axis=1)
-            dk_out[r, : taps + 1, l * LANES : l * LANES + wide] = total[:, :wide]
+        done.append(copy)
     for t in range(ticks - 1):
         for c, step in ((0, 1), (1, -1), (2, -1), (3, 1)):
             @pl.when(inside(pos + step))
             def _():
                 link(t, c, pos + step).wait_send()
-    for copy in outs:
+    if share:
+        gm_out, gk_out, gb_out = outs[2:]
+        swaps[0].wait_recv()
+        swaps[2].wait_recv()
+        mixed = mix_half(0, half) + landed[0, :share, :].astype(jnp.float32)
+        gm_out[0, 0] = (mixed + landed[2, :share, :].astype(jnp.float32)) * factor
+        rest = small_half(0, half) + landed[0, share:, :share].astype(jnp.float32)
+        rest = (rest + landed[2, share:, :share].astype(jnp.float32)) * factor
+        for a in range(side):
+            gk_out[0, 0, a] = rest[a * side : (a + 1) * side]
+        gb_out[0] = rest[taps : taps + 1]
+        for swap in swaps:
+            swap.wait_send()
+    else:
+        for r in range(2):
+            finish_small(r)
+        outs[2][...] = dp_acc[...]
+        outs[3][...] = small[...]
+    for copy in done:
         copy.wait()
 
 
-def relay(n, act, cot, new_in, loss, stored, kern, bias, mix):
+def relay(n, share, factor, act, cot, new_in, loss, stored, kern, bias, mix):
     ticks = stored.shape[1]
     height, width, chans = stored.shape[-3:]
-    side = kern.shape[-2]
+    side = kern.shape[2]
     taps = side * side
     tiles = -(-chans // LANES)
     padded = tiles * LANES
@@ -257,17 +337,20 @@
     f32, bf16 = jnp.float32, jnp.bfloat16
     vmem = pl.BlockSpec(memory_space=pltpu.VMEM)
     anywhere = pl.BlockSpec(memory_space=pl.ANY)
-    small = -(-(taps + 1) // SUB) * SUB
+    small = -(-(taps + 1) // 16) * 16
+    if share:
+        sums = [(1, 1, share, chans), (1, 1, side, side, share), (1, 1, share)]
+    else:
+        sums = [(2, chans, chans), (2, small, chans)]
     return pl.pallas_call(
-        functools.partial(relay_kernel, n),
+        functools.partial(relay_kernel, n, share, factor),
         out_shape=(
             jax.ShapeDtypeStruct(act.shape, bf16),
             jax.ShapeDtypeStruct(cot.shape, bf16),
-            jax.ShapeDtypeStruct((2, chans, chans), f32),
-            jax.ShapeDtypeStruct((2, taps + 1, chans), f32),
+            *(jax.ShapeDtypeStruct(shape, f32) for shape in sums),
         ),
-        in_specs=[anywhere] * 4 + [vmem] * 4,
-        out_specs=(anywhere, anywhere, vmem, vmem),
+        in_specs=[anywhere] * 8,
+        out_specs=(anywhere, anywhere, *(vmem for _ in sums)),
         scratch_shapes=[
             pltpu.VMEM((tiles, height, across, LANES), f32),
             pltpu.VMEM((2, tiles, height, across, LANES), f32),
@@ -278,15 +361,27 @@
             pltpu.VMEM((count, padded), f32),
             pltpu.VMEM((2, tiles, small, LANES), f32),
             pltpu.VMEM((2, tiles, taps + 1, SUB, LANES), f32),
+            pltpu.VMEM((2, chans, chans), f32),
+            pltpu.VMEM((2, small, chans), f32),
             pltpu.VMEM((ticks, 4, height, width, chans), bf16),
             pltpu.VMEM((ticks, 4, height, width, chans), bf16),
+            pltpu.VMEM(stored.shape, bf16),
+            pltpu.VMEM(kern.shape, bf16),
+            pltpu.VMEM(bias.shape, f32),
+            pltpu.VMEM(mix.shape, bf16),
+            pltpu.VMEM((3, share + small, chans), bf16),
+            pltpu.VMEM((3, share + small, chans), bf16),
             pltpu.SemaphoreType.DMA((ticks, 4)),
             pltpu.SemaphoreType.DMA((ticks, 4)),
             pltpu.SemaphoreType.DMA((ticks, 4)),
             pltpu.SemaphoreType.DMA((4,)),
+            pltpu.SemaphoreType.DMA((3,)),
+            pltpu.SemaphoreType.DMA((2, ticks)),
+            pltpu.SemaphoreType.DMA((3,)),
+            pltpu.SemaphoreType.DMA((3,)),
         ],
         compiler_params=pltpu.CompilerParams(
-            collective_id=0, has_side_effects=True, vmem_limit_bytes=40 * 1024 * 1024
+            collective_id=0, has_side_effects=True, vmem_limit_bytes=60 * 1024 * 1024
         ),
         name="relay",
     )(act, cot, new_in, loss, stored, kern, bias, mix)
@@ -296,19 +391,25 @@
     activations, stored_inputs, cotangents, new_inputs, loss_grad, depth_kernel, depth_bias, mixing
 ):
     sections = lax.axis_size("section")
+    copies = lax.axis_size("dp")
     side = depth_kernel.shape[-2]
     taps = side * side
     ticks = stored_inputs.shape[1]
-    outputs, grads, mix_sums, small_sums = relay(
-        sections, activations, cotangents, new_inputs, loss_grad,
-        stored_inputs, depth_kernel, depth_bias, mixing,
+    chans = mixing.shape[-1]
+    map_rows = activations.shape[3] * activations.shape[4]
+    factor = (2.0 * ticks * activations.shape[2] * copies * map_rows) ** (-0.5)
+    in_kernel = copies == 2 and sections % 2 == 0 and chans % 32 == 0
+    share = chans // 2 if in_kernel else 0
+    outputs, grads, *sums = relay(
+        sections, share, factor, activations, cotangents, new_inputs, loss_grad,
+        stored_inputs, depth_kernel.transpose(0, 2, 3, 4, 1, 5), depth_bias, mixing,
     )
-    mix_share = lax.psum_scatter(mix_sums, "dp", scatter_dimension=1, tiled=True)
-    small_share = lax.psum_scatter(small_sums, "dp", scatter_dimension=2, tiled=True)
+    if in_kernel:
+        return (outputs, grads, sums[1], sums[2], sums[0])
+    mix_share = lax.psum_scatter(sums[0], "dp", scatter_dimension=1, tiled=True)
+    small_share = lax.psum_scatter(sums[1], "dp", scatter_dimension=2, tiled=True)
     swap = [(i, sections - 1 - i) for i in range(sections)]
     mix_other, small_other = lax.ppermute((mix_share[1], small_share[1]), "section", swap)
-    map_rows = activations.shape[3] * activations.shape[4]
-    factor = (2.0 * ticks * activations.shape[2] * lax.axis_size("dp") * map_rows) ** (-0.5)
     grad_mixing = ((mix_share[0] + mix_other) * factor)[None, None]
     small = (small_share[0] + small_other) * factor
     grad_kernel = small[:taps].reshape(1, 1, side, side, -1)

time: 128 us -> 54.9 us (0.43)
  the two profiles are of different devices: /device:TPU:9 before, /device:TPU:17 now
where the time goes in v1:
time: 54.9 us; the launch traced here: 54.6 us
  Pallas kernels  47.4 us (86%)
  local copies, waits for them, and re-layouts  6.55 us (12%)
  between operations  0.66 us (1%)
    pallas_call x1, Pallas kernels, relay(): pl.pallas_call(functools.partial(relay_kernel, n, share, factor), out_sha...  47.4 us
    unnamed x9, local copies, waits for them, and re-layouts  6.55 us

profile of v1, /device:TPU:17, one launch (start us, length us, event | category | flops | bytes accessed | tf_op | source)
XLA Modules:
  0.0 54.6 jit_solution(16819034902811407362)
XLA Ops:
  0.6 47.4 %relay.1 = (bf16[2,1,1,8,32,416]{5,4,3,2,1,0:T(8,128)(2,1)}, bf16[2,1,1,8,32,416]{5,4,3,2,1,0:T(8,128)(2,1)}, f32[1,1,208,416]{3,2,1,0:T(8,128)}, f32[1,1,5,5,208]{4,3,2,1,0:T(8,128)}, f32[1,1,208]{2,1,0:T(1,128)}) custom-call(bf16[2,1,1,8,32,416]{5,4,3,2,1,0:T(8,128)(2,1)} %act.1, bf16[2,1,1,8,32,416]{5,4,3,2,1,0:T(8,128)(2,1)} %cot.1, ...), custom_call_target="tpu_custom_call" | custom-call | tf_op jit(solution)/shard_map/relay/pallas_call | solution.py:345
  48.0 0.0 copy-start.1
  48.1 0.0 copy-start
  48.1 1.5 %copy.13 = f32[1,1,5,5,208]{4,1,3,2,0:T(1,128)} copy(f32[1,1,5,5,208]{4,3,2,1,0:T(8,128)} %get-tuple-element.17) | data formatting | bytes 41600
  49.5 1.9 %copy.18 = bf16[2,1,1,8,32,416]{5,4,3,2,1,0:T(8,128)(2,1)} copy(bf16[2,1,1,8,32,416]{5,4,3,2,1,0:T(8,128)(2,1)} %get-tuple-element.25) | data formatting | bytes 851968
  51.4 1.9 %copy.19 = bf16[2,1,1,8,32,416]{5,4,3,2,1,0:T(8,128)(2,1)} copy(bf16[2,1,1,8,32,416]{5,4,3,2,1,0:T(8,128)(2,1)} %get-tuple-element.26) | data formatting | bytes 851968
  53.3 0.0 copy-done.1
  53.3 0.6 %copy.20 = f32[1,1,208]{2,1,0:T(1,128)} copy(f32[1,1,208]{2,1,0:T(1,128)S(1)} %copy-done.1) | data formatting | bytes 1664
  53.9 0.0 copy-done
  53.9 0.8 %copy.21 = f32[1,1,208,416]{3,2,1,0:T(8,128)} copy(f32[1,1,208,416]{3,2,1,0:T(8,128)S(1)} %copy-done) | data formatting | bytes 692224
Async XLA Ops:
  48.0 5.2 %copy-start.1 = (f32[1,1,208]{2,1,0:T(1,128)S(1)}, f32[1,1,208]{2,1,0:T(1,128)}, u32[]{:S(2)}) copy-start(f32[1,1,208]{2,1,0:T(1,128)} %get-tuple-element.28) | copy-start | bytes 2500
  48.1 5.8 %copy-start = (f32[1,1,208,416]{3,2,1,0:T(8,128)S(1)}, f32[1,1,208,416]{3,2,1,0:T(8,128)}, u32[]{:S(2)}) copy-start(f32[1,1,208,416]{3,2,1,0:T(8,128)} %get-tuple-element.29) | copy-start | bytes 1038340

commit v2 on v1

--- a/solution.py
+++ b/solution.py
@@ -21,7 +21,7 @@
     outs, refs = refs[:4 + (share > 0)], refs[4 + (share > 0):]
     y_out, dx_out = outs[:2]
     (
-        xf, xb, dpad, hid, hidb, slope, work, kw, dk_acc, dp_acc, small, rx, tx,
+        xf, xb, dpad, hid, hidb, hidden_grad, work, kw, dk_acc, dp_acc, small, rx, tx,
         stored, kern, bias, mix, parcel, landed,
         local_sem, send_sem, recv_sem, out_sem, load_sem, stored_sem, swap_send, swap_recv,
     ) = refs
@@ -37,7 +37,9 @@
 
     loads = [
         pltpu.make_async_copy(source, dest, load_sem.at[i])
-        for i, (source, dest) in enumerate(((kern_in, kern), (bias_in, bias), (mix_in, mix)))
+        for i, (source, dest) in enumerate(
+            ((kern_in, kern), (bias_in, bias), (mix_in.at[0, :, 0], mix.at[:, :chans]))
+        )
     ]
     for load in loads:
         load.start()
@@ -152,6 +154,10 @@
         def _():
             link(t, c, dst).start()
 
+    def leave(c):
+        target = (y_out if c < 2 else dx_out).at[c % 2, 0, 0]
+        return pltpu.make_async_copy(tx.at[ticks - 1, c], target, out_sem.at[c])
+
     def forward(r, t):
         arrive(t, r, pos - 1 + 2 * r)
         stage(rx.at[t, r], xf)
@@ -167,44 +173,45 @@
             return carry
 
         lax.fori_loop(0, tiles, tile, 0)
-        mixed = jnp.dot(hid[:, :chans], mix[0, r, 0], preferred_element_type=jnp.float32)
+        mixed = jnp.dot(hid[:, :chans], mix[r, :chans], preferred_element_type=jnp.float32)
         result = rx[t, r].astype(jnp.float32) + mixed.reshape(height, width, chans)
         tx[t, r] = result.astype(jnp.bfloat16)
         depart(t, r, pos + 1 - 2 * r)
+        if t == ticks - 1:
+            leave(r).start()
 
     def backward(r, t):
         pltpu.make_async_copy(stored_in.at[r, t], stored.at[r, t], stored_sem.at[r, t]).wait()
-        stage(stored.at[r, t, 0, 0], xb.at[r])
-
-        def tile(l, carry):
+        stage(stored.at[r, t, 0, 0], xb.at[r, t])
+        arrive(t, 2 + r, pos + 1 - 2 * r)
+
+        def recompute(l, carry):
+            incoming = rx[t, 2 + r].reshape(height * width, chans)
+            hidden_grad[...] = lax.dot_general(
+                incoming, mix[r, lane_tile(l)], (((1,), (1,)), ((), ())), preferred_element_type=jnp.float32
+            )
             first = jnp.broadcast_to(kw[r, l, taps : taps + 1, :], (width, LANES))
-            total = conv(xb.at[r, l], r, l, False, first)
+            total = conv(xb.at[r, t, l], r, l, False, first)
+            bias_sum = dk_acc[r, l, taps]
             for h in range(height):
                 u = total[h]
                 half = 0.5 * u
                 square = u * u
                 th = jnp.tanh(u * (GELU_A + GELU_B * square))
-                hidb[r, rows(h), lane_tile(l)] = (half + half * th).astype(jnp.bfloat16)
+                hidb[r, t, rows(h), lane_tile(l)] = (half + half * th).astype(jnp.bfloat16)
                 inner = GELU_A + (3.0 * GELU_B) * square
-                slope[l, rows(h), :] = (0.5 + 0.5 * th) + half * (1.0 - th * th) * inner
-            return carry
-
-        lax.fori_loop(0, tiles, tile, 0)
-        arrive(t, 2 + r, pos + 1 - 2 * r)
-        incoming = rx[t, 2 + r].reshape(height * width, chans)
-        work[:, :chans] = lax.dot_general(
-            incoming, mix[0, r, 0], (((1,), (1,)), ((), ())), preferred_element_type=jnp.float32
-        )
-
-        def spread(l, carry):
-            bias_sum = jnp.zeros((SUB, LANES), jnp.float32)
-            for h in range(height):
-                grad = work[rows(h), lane_tile(l)] * slope[l, rows(h), :]
-                dpad[r, l, h, SUB : SUB + width, :] = grad
+                slope = (0.5 + 0.5 * th) + half * (1.0 - th * th) * inner
+                grad = hidden_grad[rows(h), :] * slope
+                dpad[r, t, l, h, SUB : SUB + width, :] = grad
                 for w in range(0, width, SUB):
                     bias_sum = bias_sum + grad[w : w + SUB]
-            dk_acc[r, l, taps] = dk_acc[r, l, taps] + bias_sum
-            total = conv(dpad.at[r, l], r, l, True, jnp.zeros((width, LANES), jnp.float32))
+            dk_acc[r, l, taps] = bias_sum
+            return carry
+
+        lax.fori_loop(0, tiles, recompute, 0)
+
+        def spread(l, carry):
+            total = conv(dpad.at[r, t, l], r, l, True, jnp.zeros((width, LANES), jnp.float32))
             for h in range(height):
                 work[rows(h), lane_tile(l)] = total[h]
             return carry
@@ -213,19 +220,20 @@
         result = rx[t, 2 + r].astype(jnp.float32) + work[:, :chans].reshape(height, width, chans)
         tx[t, 2 + r] = result.astype(jnp.bfloat16)
         depart(t, 2 + r, pos - 1 + 2 * r)
+        if t == ticks - 1:
+            leave(2 + r).start()
 
     def weights(r, t):
-        incoming = rx[t, 2 + r].reshape(height * width, chans)
-        dp_acc[r] += lax.dot_general(
-            hidb[r, :, :chans], incoming, (((0,), (0,)), ((), ())), preferred_element_type=jnp.float32
-        )
-
         def tile(l, carry):
-            grads = [dpad[r, l, h, SUB : SUB + width, :] for h in range(height)]
+            incoming = rx[t, 2 + r].reshape(height * width, chans)
+            dp_acc[r, lane_tile(l), :] += lax.dot_general(
+                hidb[r, t, :, lane_tile(l)], incoming, (((0,), (0,)), ((), ())), preferred_element_type=jnp.float32
+            )
+            grads = [dpad[r, t, l, h, SUB : SUB + width, :] for h in range(height)]
             for b in range(side):
                 sums = [None] * side
                 for source in range(height):
-                    values = shifted(xb.at[r, l], source, b)
+                    values = shifted(xb.at[r, t, l], source, b)
                     for a in range(side):
                         h = source - a + margin
                         if 0 <= h < height:
@@ -238,6 +246,14 @@
             return carry
 
         lax.fori_loop(0, tiles, tile, 0)
+
+    def weights_of(r, start, stop):
+        def one(t, carry):
+            weights(r, t)
+            return carry
+
+        if stop > start:
+            lax.fori_loop(start, stop, one, 0)
 
     def finish_small(r):
         for l, wide in enumerate(widths):
@@ -277,27 +293,31 @@
         parcel[2, share:, :share] = rest.astype(jnp.bfloat16)
         swaps[2].start()
 
-    def tick(t, carry):
-        last = t == ticks - 1
-        for r in (1, 0):
-            backward(r, t)
-            if share and r == 0:
-                pl.when(last)(send_mirror)
-            weights(r, t)
-            if share:
-                pl.when(last)(functools.partial(send_half, r))
-        for r in (0, 1):
-            forward(r, t)
-        return carry
-
-    lax.fori_loop(0, ticks, tick, 0)
-
-    done = []
-    for c in range(4):
-        target = (y_out if c < 2 else dx_out).at[c % 2, 0, 0]
-        copy = pltpu.make_async_copy(tx.at[ticks - 1, c], target, out_sem.at[c])
-        copy.start()
-        done.append(copy)
+    last = ticks - 1
+    for t in range(last):
+        backward(1, t)
+        if t == last - 1:
+            weights_of(1, 0, last)
+        backward(0, t)
+        if t < last - 1:
+            forward(0, t)
+            forward(1, t)
+    backward(1, last)
+    weights_of(1, last, ticks)
+    if share:
+        send_half(1)
+    if last:
+        forward(0, last - 1)
+        forward(1, last - 1)
+    if share:
+        send_mirror()
+    backward(0, last)
+    weights_of(0, 0, ticks)
+    if share:
+        send_half(0)
+    forward(0, last)
+    forward(1, last)
+
     for t in range(ticks - 1):
         for c, step in ((0, 1), (1, -1), (2, -1), (3, 1)):
             @pl.when(inside(pos + step))
@@ -312,17 +332,45 @@
         rest = small_half(0, half) + landed[0, share:, :share].astype(jnp.float32)
         rest = (rest + landed[2, share:, :share].astype(jnp.float32)) * factor
         for a in range(side):
-            gk_out[0, 0, a] = rest[a * side : (a + 1) * side]
+            for b in range(side):
+                gk_out[0, a, b] = rest[a * side + b : a * side + b + 1]
         gb_out[0] = rest[taps : taps + 1]
         for swap in swaps:
             swap.wait_send()
     else:
         for r in range(2):
             finish_small(r)
-        outs[2][...] = dp_acc[...]
+        outs[2][...] = dp_acc[:, :chans]
         outs[3][...] = small[...]
-    for copy in done:
+    for c in range(4):
+        leave(c).wait()
+
+
+def place_kernel(*refs):
+    half = len(refs) // 2
+    sem = refs[-1]
+    copies = []
+    for source, dest in zip(refs[:half], refs[half:-1]):
+        parts = [(source.at[r], dest.at[r]) for r in range(2)] if source.shape[0] == 2 else [(source, dest)]
+        for one, other in parts:
+            copies.append(pltpu.make_async_copy(one, other, sem.at[len(copies)]))
+    for copy in copies:
+        copy.start()
+    for copy in copies:
         copy.wait()
+
+
+def place(results):
+    anywhere = pl.BlockSpec(memory_space=pl.ANY)
+    return pl.pallas_call(
+        place_kernel,
+        out_shape=tuple(jax.ShapeDtypeStruct(x.shape, x.dtype) for x in results),
+        in_specs=[anywhere] * len(results),
+        out_specs=tuple(anywhere for _ in results),
+        scratch_shapes=[pltpu.SemaphoreType.DMA((2 * len(results),))],
+        compiler_params=pltpu.CompilerParams(vmem_limit_bytes=60 * 1024 * 1024),
+        name="place",
+    )(*results)
 
 
 def relay(n, share, factor, act, cot, new_in, loss, stored, kern, bias, mix):
@@ -339,7 +387,7 @@
     anywhere = pl.BlockSpec(memory_space=pl.ANY)
     small = -(-(taps + 1) // 16) * 16
     if share:
-        sums = [(1, 1, share, chans), (1, 1, side, side, share), (1, 1, share)]
+        sums = [(1, 1, share, chans), (1, side, side, 1, share), (1, 1, share)]
     else:
         sums = [(2, chans, chans), (2, small, chans)]
     return pl.pallas_call(
@@ -353,22 +401,22 @@
         out_specs=(anywhere, anywhere, *(vmem for _ in sums)),
         scratch_shapes=[
             pltpu.VMEM((tiles, height, across, LANES), f32),
-            pltpu.VMEM((2, tiles, height, across, LANES), f32),
-            pltpu.VMEM((2, tiles, height, across, LANES), f32),
+            pltpu.VMEM((2, ticks, tiles, height, across, LANES), f32),
+            pltpu.VMEM((2, ticks, tiles, height, across, LANES), f32),
             pltpu.VMEM((count, padded), bf16),
-            pltpu.VMEM((2, count, padded), bf16),
-            pltpu.VMEM((tiles, count, LANES), f32),
+            pltpu.VMEM((2, ticks, count, padded), bf16),
+            pltpu.VMEM((count, LANES), f32),
             pltpu.VMEM((count, padded), f32),
             pltpu.VMEM((2, tiles, small, LANES), f32),
             pltpu.VMEM((2, tiles, taps + 1, SUB, LANES), f32),
-            pltpu.VMEM((2, chans, chans), f32),
+            pltpu.VMEM((2, padded, chans), f32),
             pltpu.VMEM((2, small, chans), f32),
             pltpu.VMEM((ticks, 4, height, width, chans), bf16),
             pltpu.VMEM((ticks, 4, height, width, chans), bf16),
             pltpu.VMEM(stored.shape, bf16),
             pltpu.VMEM(kern.shape, bf16),
             pltpu.VMEM(bias.shape, f32),
-            pltpu.VMEM(mix.shape, bf16),
+            pltpu.VMEM((2, padded, chans), bf16),
             pltpu.VMEM((3, share + small, chans), bf16),
             pltpu.VMEM((3, share + small, chans), bf16),
             pltpu.SemaphoreType.DMA((ticks, 4)),
@@ -405,7 +453,8 @@
         stored_inputs, depth_kernel.transpose(0, 2, 3, 4, 1, 5), depth_bias, mixing,
     )
     if in_kernel:
-        return (outputs, grads, sums[1], sums[2], sums[0])
+        outputs, grads, grad_mixing, grad_kernel, grad_bias = place((outputs, grads, *sums))
+        return (outputs, grads, grad_kernel.transpose(0, 3, 1, 2, 4), grad_bias, grad_mixing)
     mix_share = lax.psum_scatter(sums[0], "dp", scatter_dimension=1, tiled=True)
     small_share = lax.psum_scatter(sums[1], "dp", scatter_dimension=2, tiled=True)
     swap = [(i, sections - 1 - i) for i in range(sections)]

time: 54.9 us -> 93.7 us (1.71)
  the two profiles are of different devices: /device:TPU:17 before, /device:TPU:0 now
where the time goes in v2:
time: 93.7 us; the launch traced here: 92.4 us
  Pallas kernels  91.7 us (98%)
    pallas_call x1, Pallas kernels, place(): pl.pallas_call(place_kernel, out_shape=tuple((jax.ShapeDtypeStruct(x.shap...  46.7 us
    pallas_call x1, Pallas kernels, relay(): pl.pallas_call(functools.partial(relay_kernel, n, share, factor), out_sha...  45.1 us

profile of v2, /device:TPU:0, one launch (start us, length us, event | category | flops | bytes accessed | tf_op | source)
XLA Modules:
  0.0 92.4 jit_solution(18177218680057710266)
XLA Ops:
  0.6 45.1 %relay.1 = (bf16[2,1,1,8,32,416]{5,4,3,2,1,0:T(8,128)(2,1)}, bf16[2,1,1,8,32,416]{5,4,3,2,1,0:T(8,128)(2,1)}, f32[1,1,208,416]{3,2,1,0:T(8,128)}, f32[1,5,5,1,208]{4,3,2,1,0:T(1,128)}, f32[1,1,208]{2,1,0:T(1,128)}) custom-call(bf16[2,1,1,8,32,416]{5,4,3,2,1,0:T(8,128)(2,1)} %act.1, bf16[2,1,1,8,32,416]{5,4,3,2,1,0:T(8,128)(2,1)} %cot.1, ...), custom_call_target="tpu_custom_call" | custom-call | tf_op jit(solution)/shard_map/relay/pallas_call | solution.py:393
  45.7 46.7 %place.1 = (bf16[2,1,1,8,32,416]{5,4,3,2,1,0:T(8,128)(2,1)}, bf16[2,1,1,8,32,416]{5,4,3,2,1,0:T(8,128)(2,1)}, f32[1,1,208,416]{3,2,1,0:T(8,128)}, f32[1,5,5,1,208]{4,3,2,1,0:T(1,128)}, f32[1,1,208]{2,1,0:T(1,128)}) custom-call(bf16[2,1,1,8,32,416]{5,4,3,2,1,0:T(8,128)(2,1)} %get-tuple-element.15.refs_0_, ...), custom_call_target="tpu_custom_call" | custom-call | tf_op jit(solution)/shard_map/place/pallas_call | solution.py:365

commit v3 on v2

--- a/solution.py
+++ b/solution.py
@@ -21,7 +21,7 @@
     outs, refs = refs[:4 + (share > 0)], refs[4 + (share > 0):]
     y_out, dx_out = outs[:2]
     (
-        xf, xb, dpad, hid, hidb, hidden_grad, work, kw, dk_acc, dp_acc, small, rx, tx,
+        xf, xb, dpad, hid, hidb, hidden_grad, work, kw, dk_acc, dp_acc, small, rx, tx, mail_in, mail_out,
         stored, kern, bias, mix, parcel, landed,
         local_sem, send_sem, recv_sem, out_sem, load_sem, stored_sem, swap_send, swap_recv,
     ) = refs
@@ -120,8 +120,8 @@
 
     def link(t, c, dst):
         return pltpu.make_async_remote_copy(
-            src_ref=tx.at[t, c],
-            dst_ref=rx.at[t + 1, c],
+            src_ref=mail_out.at[t, c],
+            dst_ref=mail_in.at[t, c],
             send_sem=send_sem.at[t, c],
             recv_sem=recv_sem.at[t + 1, c],
             device_id={"section": dst},
@@ -131,27 +131,66 @@
     def inside(place):
         return jnp.logical_and(place >= 0, place < n)
 
+    whole, rest = divmod(chans, LANES)
+    count = height * width
+    groups = fold_groups(chans, height)
+    group_rows = count // groups
+
+    def pack(c, t):
+        for l in range(whole):
+            mail_out[t, c, l * count : (l + 1) * count, :] = tx[
+                t, c, :, :, l * LANES : (l + 1) * LANES
+            ].reshape(count, LANES)
+        if rest:
+            ends = tx[t, c, :, :, whole * LANES :].reshape(count, rest).astype(jnp.float32)
+            parts = [ends[g * group_rows : (g + 1) * group_rows] for g in range(groups)]
+            folded = jnp.concatenate(parts, axis=1).astype(jnp.bfloat16)
+            mail_out[t, c, whole * count :, : groups * rest] = folded
+
+    def unpack(c, t):
+        for l in range(whole):
+            rx[t, c, :, :, l * LANES : (l + 1) * LANES] = mail_in[
+                t - 1, c, l * count : (l + 1) * count, :
+            ].reshape(height, width, LANES)
+        if rest:
+            folded = mail_in[t - 1, c, whole * count :, :].astype(jnp.float32)
+            for g in range(groups):
+                part = folded[:, g * rest : (g + 1) * rest].astype(jnp.bfloat16)
+                rx[t, c, g * height // groups : (g + 1) * height // groups, :, whole * LANES :] = part.reshape(
+                    height // groups, width, rest
+                )
+
     def arrive(t, c, src):
-        remote = jnp.logical_and(t > 0, inside(src))
-
-        @pl.when(remote)
+        def local():
+            pltpu.make_async_copy(act.at[0, 0, 0], rx.at[t, c], local_sem.at[t, c]).wait()
+
+        if t == 0:
+            local()
+            return
+
+        @pl.when(inside(src))
         def _():
             pltpu.make_async_remote_copy(
-                src_ref=tx.at[t, c],
-                dst_ref=rx.at[t, c],
-                send_sem=send_sem.at[t, c],
+                src_ref=mail_out.at[t - 1, c],
+                dst_ref=mail_in.at[t - 1, c],
+                send_sem=send_sem.at[t - 1, c],
                 recv_sem=recv_sem.at[t, c],
                 device_id={"section": left},
                 device_id_type=MESH,
             ).wait_recv()
-
-        @pl.when(jnp.logical_not(remote))
+            unpack(c, t)
+
+        @pl.when(jnp.logical_not(inside(src)))
         def _():
-            pltpu.make_async_copy(act.at[0, 0, 0], rx.at[t, c], local_sem.at[t, c]).wait()
+            local()
 
     def depart(t, c, dst):
-        @pl.when(jnp.logical_and(t < ticks - 1, inside(dst)))
+        if t == ticks - 1:
+            return
+
+        @pl.when(inside(dst))
         def _():
+            pack(c, t)
             link(t, c, dst).start()
 
     def leave(c):
@@ -279,40 +318,69 @@
     def small_half(r, which):
         return jnp.where(which == 0, small[r, :, :share], small[r, :, share:])
 
+    share_whole = chans // LANES
+    rest_rows = parcel_rest_rows(share, chans)
+    bulk = share_whole * share
+    small_rows = small.shape[1]
+
+    def fill(i, mixed, ends):
+        for l in range(share_whole):
+            parcel[i, l * share : (l + 1) * share, :] = mixed[:, l * LANES : (l + 1) * LANES].astype(jnp.bfloat16)
+        if rest_rows:
+            for g in range(-(-share // rest_rows)):
+                part = mixed[g * rest_rows : (g + 1) * rest_rows, share_whole * LANES :]
+                parcel[i, bulk : bulk + part.shape[0], g * rest : (g + 1) * rest] = part.astype(jnp.bfloat16)
+        for l in range(-(-share // LANES)):
+            part = ends[:, l * LANES : (l + 1) * LANES]
+            start = bulk + rest_rows + l * small_rows
+            parcel[i, start : start + small_rows, : part.shape[1]] = part.astype(jnp.bfloat16)
+        swaps[i].start()
+
+    def opened(i):
+        mixed = [landed[i, l * share : (l + 1) * share, :] for l in range(share_whole)]
+        if rest_rows:
+            parts = []
+            for g in range(-(-share // rest_rows)):
+                wanted = min(rest_rows, share - g * rest_rows)
+                parts.append(landed[i, bulk : bulk + wanted, :].astype(jnp.float32)[:, g * rest : (g + 1) * rest])
+            mixed.append(jnp.concatenate(parts, axis=0))
+        ends = []
+        for l in range(-(-share // LANES)):
+            start = bulk + rest_rows + l * small_rows
+            ends.append(landed[i, start : start + small_rows, : min(LANES, share - l * LANES)])
+        return tuple(
+            jnp.concatenate([x.astype(jnp.float32) for x in parts], axis=1) for parts in (mixed, ends)
+        )
+
     def send_half(r):
         finish_small(r)
-        parcel[r, :share, :] = mix_half(r, 1 - half).astype(jnp.bfloat16)
-        parcel[r, share:, :share] = small_half(r, 1 - half).astype(jnp.bfloat16)
-        swaps[r].start()
+        fill(r, mix_half(r, 1 - half), small_half(r, 1 - half))
 
     def send_mirror():
         swaps[1].wait_recv()
-        mixed = mix_half(1, half) + landed[1, :share, :].astype(jnp.float32)
-        parcel[2, :share, :] = mixed.astype(jnp.bfloat16)
-        rest = small_half(1, half) + landed[1, share:, :share].astype(jnp.float32)
-        parcel[2, share:, :share] = rest.astype(jnp.bfloat16)
-        swaps[2].start()
+        mixed, ends = opened(1)
+        fill(2, mix_half(1, half) + mixed, small_half(1, half) + ends)
 
     last = ticks - 1
     for t in range(last):
         backward(1, t)
-        if t == last - 1:
-            weights_of(1, 0, last)
+        forward(0, t)
+        forward(1, t)
+        if t:
+            weights(1, t - 1)
         backward(0, t)
-        if t < last - 1:
-            forward(0, t)
-            forward(1, t)
+    if last:
+        weights(1, last - 1)
     backward(1, last)
-    weights_of(1, last, ticks)
+    weights(1, last)
     if share:
         send_half(1)
-    if last:
-        forward(0, last - 1)
-        forward(1, last - 1)
+    weights_of(0, 0, min(1, last))
     if share:
         send_mirror()
+    weights_of(0, min(1, last), last)
     backward(0, last)
-    weights_of(0, 0, ticks)
+    weights(0, last)
     if share:
         send_half(0)
     forward(0, last)
@@ -327,14 +395,13 @@
         gm_out, gk_out, gb_out = outs[2:]
         swaps[0].wait_recv()
         swaps[2].wait_recv()
-        mixed = mix_half(0, half) + landed[0, :share, :].astype(jnp.float32)
-        gm_out[0, 0] = (mixed + landed[2, :share, :].astype(jnp.float32)) * factor
-        rest = small_half(0, half) + landed[0, share:, :share].astype(jnp.float32)
-        rest = (rest + landed[2, share:, :share].astype(jnp.float32)) * factor
+        near, far = opened(0), opened(2)
+        gm_out[0, 0] = (mix_half(0, half) + near[0] + far[0]) * factor
+        ends = (small_half(0, half) + near[1] + far[1]) * factor
         for a in range(side):
             for b in range(side):
-                gk_out[0, a, b] = rest[a * side + b : a * side + b + 1]
-        gb_out[0] = rest[taps : taps + 1]
+                gk_out[0, a, b] = ends[a * side + b : a * side + b + 1]
+        gb_out[0] = ends[taps : taps + 1]
         for swap in swaps:
             swap.wait_send()
     else:
@@ -347,17 +414,26 @@
 
 
 def place_kernel(*refs):
-    half = len(refs) // 2
-    sem = refs[-1]
-    copies = []
-    for source, dest in zip(refs[:half], refs[half:-1]):
-        parts = [(source.at[r], dest.at[r]) for r in range(2)] if source.shape[0] == 2 else [(source, dest)]
-        for one, other in parts:
-            copies.append(pltpu.make_async_copy(one, other, sem.at[len(copies)]))
-    for copy in copies:
-        copy.start()
-    for copy in copies:
-        copy.wait()
+    half = len(refs) // 3
+    sources, targets, held = refs[:half], refs[half : 2 * half], refs[2 * half : 3 * half]
+    in_sem, out_sem = refs[3 * half :]
+    trips = []
+    for trio in zip(sources, held, targets):
+        for source, stop, target in [[x.at[r] for x in trio] for r in range(2)] if trio[0].shape[0] == 2 else [trio]:
+            i = len(trips)
+            trips.append(
+                (
+                    pltpu.make_async_copy(source, stop, in_sem.at[i]),
+                    pltpu.make_async_copy(stop, target, out_sem.at[i]),
+                )
+            )
+    for fetch, _ in trips:
+        fetch.start()
+    for fetch, put in trips:
+        fetch.wait()
+        put.start()
+    for _, put in trips:
+        put.wait()
 
 
 def place(results):
@@ -367,10 +443,27 @@
         out_shape=tuple(jax.ShapeDtypeStruct(x.shape, x.dtype) for x in results),
         in_specs=[anywhere] * len(results),
         out_specs=tuple(anywhere for _ in results),
-        scratch_shapes=[pltpu.SemaphoreType.DMA((2 * len(results),))],
+        scratch_shapes=[
+            *(pltpu.VMEM(x.shape, x.dtype) for x in results),
+            pltpu.SemaphoreType.DMA((2 * len(results),)),
+            pltpu.SemaphoreType.DMA((2 * len(results),)),
+        ],
         compiler_params=pltpu.CompilerParams(vmem_limit_bytes=60 * 1024 * 1024),
         name="place",
     )(*results)
+
+
+def fold_groups(chans, height):
+    rest = chans % LANES
+    groups = LANES // rest if rest else 1
+    return groups if height % groups == 0 else 1
+
+
+def parcel_rest_rows(share, chans):
+    rest = chans % LANES
+    if not rest:
+        return 0
+    return -(-share // (LANES // rest * 16)) * 16
 
 
 def relay(n, share, factor, act, cot, new_in, loss, stored, kern, bias, mix):
@@ -386,6 +479,10 @@
     vmem = pl.BlockSpec(memory_space=pltpu.VMEM)
     anywhere = pl.BlockSpec(memory_space=pl.ANY)
     small = -(-(taps + 1) // 16) * 16
+    mail = chans // LANES * count
+    if chans % LANES:
+        mail += count // fold_groups(chans, height)
+    parcel = chans // LANES * share + parcel_rest_rows(share, chans) + -(-share // LANES) * small
     if share:
         sums = [(1, 1, share, chans), (1, side, side, 1, share), (1, 1, share)]
     else:
@@ -413,12 +510,14 @@
             pltpu.VMEM((2, small, chans), f32),
             pltpu.VMEM((ticks, 4, height, width, chans), bf16),
             pltpu.VMEM((ticks, 4, height, width, chans), bf16),
+            pltpu.VMEM((max(ticks - 1, 1), 4, mail, LANES), bf16),
+            pltpu.VMEM((max(ticks - 1, 1), 4, mail, LANES), bf16),
             pltpu.VMEM(stored.shape, bf16),
             pltpu.VMEM(kern.shape, bf16),
             pltpu.VMEM(bias.shape, f32),
             pltpu.VMEM((2, padded, chans), bf16),
-            pltpu.VMEM((3, share + small, chans), bf16),
-            pltpu.VMEM((3, share + small, chans), bf16),
+            pltpu.VMEM((3, parcel, LANES), bf16),
+            pltpu.VMEM((3, parcel, LANES), bf16),
             pltpu.SemaphoreType.DMA((ticks, 4)),
             pltpu.SemaphoreType.DMA((ticks, 4)),
             pltpu.SemaphoreType.DMA((ticks, 4)),

time: 93.7 us -> 48 us (0.51); the launches traced: 92.4 us -> 47.9 us
  Pallas kernels: 91.7 us -> 47.2 us
    pallas_call x1, Pallas kernels: 46.7 us -> 2.26 us  [place(): pl.pallas_call(place_kernel, out_shape=tuple((jax.ShapeDtypeStruct(x.shap...]
where the time goes in v3:
time: 48 us; the launch traced here: 47.9 us
  Pallas kernels  47.2 us (98%)
  between operations  0.64 us (1%)
    pallas_call x1, Pallas kernels, relay(): pl.pallas_call(functools.partial(relay_kernel, n, share, factor), out_sha...  45 us
    pallas_call x1, Pallas kernels, place(): pl.pallas_call(place_kernel, out_shape=tuple((jax.ShapeDtypeStruct(x.shap...  2.26 us

profile of v3, /device:TPU:0, one launch (start us, length us, event | category | flops | bytes accessed | tf_op | source)
XLA Modules:
  0.0 47.9 jit_solution(6612706190864476700)
XLA Ops:
  0.6 45.0 %relay.1 = (bf16[2,1,1,8,32,416]{5,4,3,2,1,0:T(8,128)(2,1)}, bf16[2,1,1,8,32,416]{5,4,3,2,1,0:T(8,128)(2,1)}, f32[1,1,208,416]{3,2,1,0:T(8,128)}, f32[1,5,5,1,208]{4,3,2,1,0:T(1,128)}, f32[1,1,208]{2,1,0:T(1,128)}) custom-call(bf16[2,1,1,8,32,416]{5,4,3,2,1,0:T(8,128)(2,1)} %act.1, bf16[2,1,1,8,32,416]{5,4,3,2,1,0:T(8,128)(2,1)} %cot.1, ...), custom_call_target="tpu_custom_call" | custom-call | tf_op jit(solution)/shard_map/relay/pallas_call | solution.py:490
  45.6 2.3 %place.1 = (bf16[2,1,1,8,32,416]{5,4,3,2,1,0:T(8,128)(2,1)}, bf16[2,1,1,8,32,416]{5,4,3,2,1,0:T(8,128)(2,1)}, f32[1,1,208,416]{3,2,1,0:T(8,128)}, f32[1,5,5,1,208]{4,3,2,1,0:T(1,128)}, f32[1,1,208]{2,1,0:T(1,128)}) custom-call(bf16[2,1,1,8,32,416]{5,4,3,2,1,0:T(8,128)(2,1)} %get-tuple-element.15.refs_0_, ...), custom_call_target="tpu_custom_call" | custom-call | tf_op jit(solution)/shard_map/place/pallas_call | solution.py:441

commit v4 on v3

--- a/solution.py
+++ b/solution.py
@@ -86,7 +86,6 @@
     for l, wide in enumerate(widths):
         for r in range(2):
             kw[r, l, taps : taps + 1, :wide] = bias[0, r, :, l * LANES : l * LANES + wide]
-    pl.semaphore_wait(barrier, len(greeted))
 
     def stage(source, dest):
         for l, wide in enumerate(widths):
@@ -258,6 +257,8 @@
         lax.fori_loop(0, tiles, spread, 0)
         result = rx[t, 2 + r].astype(jnp.float32) + work[:, :chans].reshape(height, width, chans)
         tx[t, 2 + r] = result.astype(jnp.bfloat16)
+        if (r, t) == (1, 0):
+            pl.semaphore_wait(barrier, len(greeted))
         depart(t, 2 + r, pos - 1 + 2 * r)
         if t == ticks - 1:
             leave(2 + r).start()
@@ -375,10 +376,9 @@
     weights(1, last)
     if share:
         send_half(1)
-    weights_of(0, 0, min(1, last))
+    weights_of(0, 0, last)
     if share:
         send_mirror()
-    weights_of(0, min(1, last), last)
     backward(0, last)
     weights(0, last)
     if share:

time: 48 us -> 45.3 us (0.944); the launches traced: 47.9 us -> 44.5 us
  Pallas kernels: 47.2 us -> 43.9 us
    pallas_call x1, Pallas kernels: 45 us -> 41.6 us  [relay(): pl.pallas_call(functools.partial(relay_kernel, n, share, factor), out_sha...]
where the time goes in v4:
time: 45.3 us; the launch traced here: 44.5 us
  Pallas kernels  43.9 us (97%)
  between operations  0.64 us (1%)
    pallas_call x1, Pallas kernels, relay(): pl.pallas_call(functools.partial(relay_kernel, n, share, factor), out_sha...  41.6 us
    pallas_call x1, Pallas kernels, place(): pl.pallas_call(place_kernel, out_shape=tuple((jax.ShapeDtypeStruct(x.shap...  2.26 us

profile of v4, /device:TPU:0, one launch (start us, length us, event | category | flops | bytes accessed | tf_op | source)
XLA Modules:
  0.0 44.5 jit_solution(8444133241260679293)
XLA Ops:
  0.6 41.6 %relay.1 = (bf16[2,1,1,8,32,416]{5,4,3,2,1,0:T(8,128)(2,1)}, bf16[2,1,1,8,32,416]{5,4,3,2,1,0:T(8,128)(2,1)}, f32[1,1,208,416]{3,2,1,0:T(8,128)}, f32[1,5,5,1,208]{4,3,2,1,0:T(1,128)}, f32[1,1,208]{2,1,0:T(1,128)}) custom-call(bf16[2,1,1,8,32,416]{5,4,3,2,1,0:T(8,128)(2,1)} %act.1, bf16[2,1,1,8,32,416]{5,4,3,2,1,0:T(8,128)(2,1)} %cot.1, ...), custom_call_target="tpu_custom_call" | custom-call | tf_op jit(solution)/shard_map/relay/pallas_call | solution.py:490
  42.2 2.3 %place.1 = (bf16[2,1,1,8,32,416]{5,4,3,2,1,0:T(8,128)(2,1)}, bf16[2,1,1,8,32,416]{5,4,3,2,1,0:T(8,128)(2,1)}, f32[1,1,208,416]{3,2,1,0:T(8,128)}, f32[1,5,5,1,208]{4,3,2,1,0:T(1,128)}, f32[1,1,208]{2,1,0:T(1,128)}) custom-call(bf16[2,1,1,8,32,416]{5,4,3,2,1,0:T(8,128)(2,1)} %get-tuple-element.15.refs_0_, ...), custom_call_target="tpu_custom_call" | custom-call | tf_op jit(solution)/shard_map/place/pallas_call | solution.py:441
